TPU v7x, 1024 devices: a whole 8x8x8 slice. The times are simulated.
1024 devices in a mesh: gx: 64 (over z, x), gy: 16 (over y, core).
Axes of the slice: x: 8, y: 8, z: 8, core: 2. Of those that a mesh axis runs over, the one named last changes fastest.
Arguments:
- background: float32 [2048, 16, 2048], P('gx', None, 'gy'), may hold values from -6 to 6
- nearbody: float32 [2, 1024, 16, 2048], P(None, 'gx', None, 'gy'), may hold values from -6 to 6
- donor_rows: int32 [64, 16, 64, 2], P('gx', 'gy'), may hold values from -1 to 479, as said below
- donor_fractions: float32 [3, 64, 16, 64, 2], P(None, 'gx', 'gy'), may hold values from 0 to 1
- fringe_slots: int32 [64, 16, 64, 2], P('gx', 'gy'), may hold values from -1 to 511, as said below
- return_rows: int32 [64, 16, 64, 2], P('gx', 'gy'), may hold values from -1 to 415, as said below
- return_fractions: float32 [3, 64, 16, 64, 2], P(None, 'gx', 'gy'), may hold values from 0 to 1
- hole_slots: int32 [64, 16, 64, 2], P('gx', 'gy'), may hold values from -1 to 511, as said below
Outputs:
- back_field: float32 [2048, 16, 2048], P('gx', None, 'gy')
- body_field: float32 [2, 1024, 16, 2048], P(None, 'gx', None, 'gy')
Inputs may be any that keep to these rules, and one draw needn't show every extreme that they name: Entry [q, j, p, s] is -1 where the slot is empty, else a row index. For each owner p and column j the sources with nonempty slots each fill exactly all 2 slots, and there are 32 of them; donor_rows[q, j, p, s] >= 0 exactly where fringe_slots[p, j, q, s] >= 0. `fringe_slots`: entry [p, j, q, s] is -1 or a fringe row (g * 16 + i) * 16 + k with k one of the two outermost layers 14, 15; every one of these 64 rows of a device appears exactly once. Entry [p, j, q, s] is -1 where the slot is empty, else a row index. For each background owner q and column j the sources with nonempty slots each fill exactly all 2 slots, and there are 32 of them; return_rows[p, j, q, s] >= 0 exactly where hole_slots[q, j, p, s] >= 0. `hole_slots`: entry [q, j, p, s] is -1 or a background row x 16 + z of the device; each device receives exactly 64 distinct rows.
All inputs are finite; a program needn't handle non-finite values.
Results may differ from a plain program's by a relative error of at most 0.0003.
Values sent between devices are 32-bit elements; how exact they have to be, the bound alone decides.
A program may use at most 32 MiB of HBM per device.

v0:
```python
import jax
import jax.numpy as jnp
from jax import lax
from jax.sharding import PartitionSpec as P

STEPS = 2


back_courant = (0.3, 0.25, 0.15)
back_diffuse = 0.04
body_courant = (0.2, 0.3, 0.2)
body_diffuse = 0.045


def extended(array, sides, width, wrap):
    for axis, dim in sides:
        devices, length = (lax.axis_size(axis), array.shape[dim])
        up = [(i, (i + 1) % devices) for i in range(devices if wrap else devices - 1)]
        down = [(j, i) for i, j in up]
        last = lax.slice_in_dim(array, length - width, length, axis=dim)
        initial = lax.slice_in_dim(array, 0, width, axis=dim)
        before = lax.ppermute(last, axis, up)
        after = lax.ppermute(initial, axis, down)
        array = jnp.concatenate([before, array, after], axis=dim)
    return array


def advance(padded, courant, diffuse):
    centre = padded[..., 1:-1, 1:-1, 1:-1]
    back_x = padded[..., :-2, 1:-1, 1:-1]
    ahead_x = padded[..., 2:, 1:-1, 1:-1]
    back_z = padded[..., 1:-1, :-2, 1:-1]
    ahead_z = padded[..., 1:-1, 2:, 1:-1]
    back_y = padded[..., 1:-1, 1:-1, :-2]
    ahead_y = padded[..., 1:-1, 1:-1, 2:]
    upwind = (
        courant[0] * (centre - back_x)
        + courant[1] * (centre - back_y)
        + courant[2] * (centre - back_z)
    )
    spread = back_x + ahead_x + back_y + ahead_y + back_z + ahead_z - 6.0 * centre
    return centre - upwind + diffuse * spread


def trilinear(field, first_row, second_row, fraction_a, fraction_b, fraction_y, row_length):
    blended = None
    for shift_a in (0, 1):
        weight_a = fraction_a if shift_a else 1.0 - fraction_a
        for shift_b in (0, 1):
            weight_b = fraction_b if shift_b else 1.0 - fraction_b
            picked = field[first_row + shift_a, second_row + shift_b]
            below_y = picked[..., 1 : row_length + 1]
            above_y = picked[..., 2 : row_length + 2]
            portion = (weight_a * weight_b)[..., None] * (
                (1.0 - fraction_y)[..., None] * below_y + fraction_y[..., None] * above_y
            )
            blended = portion if blended is None else blended + portion
    return blended


def per_device(
    background,
    nearbody,
    donor_rows,
    donor_fractions,
    fringe_slots,
    return_rows,
    return_fractions,
    hole_slots,
):
    slab_cells, plane_cells, span_cells = background.shape
    cycle_cells = nearbody.shape[1]
    layer_cells = nearbody.shape[2]
    layers_used = layer_cells - 3
    donor_index = jnp.maximum(donor_rows[0, 0], 0)
    donor_share = donor_fractions[:, 0, 0]
    return_index = jnp.maximum(return_rows[0, 0], 0)
    return_share = return_fractions[:, 0, 0]
    donor_first = donor_index // (plane_cells - 1) + 1
    donor_second = donor_index % (plane_cells - 1)
    return_first = (
        return_index // (cycle_cells * layers_used) * (cycle_cells + 2)
        + return_index // layers_used % cycle_cells
        + 1
    )
    return_second = return_index % layers_used
    body_rows = 2 * cycle_cells * layer_cells
    back_rows = slab_cells * plane_cells
    fringe_index = fringe_slots[0, 0]
    hole_index = hole_slots[0, 0]
    fringe_spot = jnp.where(fringe_index >= 0, fringe_index, body_rows).reshape(-1)
    hole_spot = jnp.where(hole_index >= 0, hole_index, back_rows).reshape(-1)
    back_field = background
    body_field = nearbody
    for repeat in range(STEPS):
        back_halo = extended(back_field, (("gx", 0), ("gy", 2)), 1, False)
        body_halo = extended(body_field, (("gx", 1), ("gy", 3)), 1, True)
        donor_values = trilinear(
            back_halo,
            donor_first,
            donor_second,
            donor_share[0],
            donor_share[1],
            donor_share[2],
            span_cells,
        )
        flat_body = body_halo.reshape(2 * (cycle_cells + 2), layer_cells, span_cells + 2)
        return_values = trilinear(
            flat_body,
            return_first,
            return_second,
            return_share[0],
            return_share[1],
            return_share[2],
            span_cells,
        )
        donor_arrived = lax.all_to_all(donor_values, "gx", split_axis=0, concat_axis=0, tiled=True)
        return_arrived = lax.all_to_all(
            return_values, "gx", split_axis=0, concat_axis=0, tiled=True
        )
        moved_back = advance(
            jnp.pad(back_halo, ((0, 0), (1, 1), (0, 0))), back_courant, back_diffuse
        )
        moved_body = advance(
            jnp.pad(body_halo, ((0, 0), (0, 0), (1, 1), (0, 0))), body_courant, body_diffuse
        )
        back_field = (
            moved_back.reshape(back_rows, span_cells)
            .at[hole_spot]
            .set(return_arrived.reshape(-1, span_cells), mode="drop")
            .reshape(slab_cells, plane_cells, span_cells)
        )
        body_field = (
            moved_body.reshape(body_rows, span_cells)
            .at[fringe_spot]
            .set(donor_arrived.reshape(-1, span_cells), mode="drop")
            .reshape(2, cycle_cells, layer_cells, span_cells)
        )
    return (back_field, body_field)


def solution(mesh):
    placed = (
        P("gx", None, "gy"),
        P(None, "gx", None, "gy"),
        P("gx", "gy", None, None),
        P(None, "gx", "gy", None, None),
        P("gx", "gy", None, None),
        P("gx", "gy", None, None),
        P(None, "gx", "gy", None, None),
        P("gx", "gy", None, None),
    )
    return jax.shard_map(
        per_device,
        mesh=mesh,
        in_specs=placed,
        out_specs=(P("gx", None, "gy"), P(None, "gx", None, "gy")),
        check_vma=False,
    )
```

profile of v0, /device:TPU:64, one launch (start us, length us, event | category | flops | bytes accessed | tf_op | source)
XLA Modules:
  0.0 176.5 jit_solution(3068459072281140618)
XLA Ops:
  1.4 1.3 collective-permute-start.1
  2.7 4.5 %collective-permute-start = (f32[1,16,128]{2,1,0:T(8,128)S(1)}, f32[1,16,128]{2,1,0:T(8,128)S(1)}, u32[]{:S(2)}, u32[]{:S(2)}) collective-permute-start(f32[1,16,128]{2,1,0:T(8,128)S(1)} %get-tuple-element.21), channel_id=1, source_target_pairs={{0,16},{16,32},{32,48},{48,64},{64,80},{80,96},{96,112},{112,128},... | collective-permute-start | bytes 24584 | tf_op jit(solution)/shard_map/ppermute | solution.py:22
  8.0 18.4 %collective-permute-start.5 = (f32[2,1,16,128]{3,2,1,0:T(8,128)S(1)}, f32[2,1,16,128]{3,2,1,0:T(8,128)S(1)}, u32[]{:S(2)}, u32[]{:S(2)}) collective-permute-start(f32[2,1,16,128]{3,2,1,0:T(8,128)S(1)} %get-tuple-element.18), channel_id=1, source_target_pairs={{16,0},{32,16},{48,32},{64,48},{80,64},{96,80},{112,96},{128,112},... | collective-permute-start | bytes 49160 | tf_op jit(solution)/shard_map/ppermute | solution.py:23
  26.4 1.9 %collective-permute-start.4 = (f32[2,1,16,128]{3,2,1,0:T(8,128)S(1)}, f32[2,1,16,128]{3,2,1,0:T(8,128)S(1)}, u32[]{:S(2)}, u32[]{:S(2)}) collective-permute-start(f32[2,1,16,128]{3,2,1,0:T(8,128)S(1)} %get-tuple-element.19), channel_id=1, source_target_pairs={{0,16},{16,32},{32,48},{48,64},{64,80},{80,96},{96,112},{112,128},... | collective-permute-start | bytes 49160 | tf_op jit(solution)/shard_map/ppermute | solution.py:22
  37.2 1.9 %collective-permute-start.2 = (f32[34,16,1]{2,1,0:T(8,128)S(1)}, f32[34,16,1]{2,1,0:T(8,128)S(1)}, u32[]{:S(2)}, u32[]{:S(2)}) collective-permute-start(f32[34,16,1]{2,1,0:T(8,128)S(1)} %get-tuple-element.12), channel_id=1, source_target_pairs={{0,1},{1,2},{2,3},{3,4},{4,5},{5,6},{6,7},{7,8},{8,9},{9,10},{10,1... | collective-permute-start | bytes 6536 | tf_op jit(solution)/shard_map/ppermute | solution.py:22
  39.1 4.9 %collective-permute-start.3 = (f32[34,16,1]{2,1,0:T(8,128)S(1)}, f32[34,16,1]{2,1,0:T(8,128)S(1)}, u32[]{:S(2)}, u32[]{:S(2)}) collective-permute-start(f32[34,16,1]{2,1,0:T(8,128)S(1)} %get-tuple-element.13), channel_id=1, source_target_pairs={{1,0},{2,1},{3,2},{4,3},{5,4},{6,5},{7,6},{8,7},{9,8},{10,9},{11,1... | collective-permute-start | bytes 6536 | tf_op jit(solution)/shard_map/ppermute | solution.py:23
  52.3 1.3 gather_fusion.4
  53.8 1.6 fusion.80
  55.4 9.3 %all-to-all-start.1 = ((f32[64,2,128]{2,1,0:T(2,128)}), f32[64,2,128]{2,1,0:T(2,128)}, u32[]{:S(2)}, u32[]{:S(2)}) async-start(f32[64,2,128]{2,1,0:T(2,128)} %fusion.80), calls=%async_computation.1 | async-start | bytes 131072 | tf_op jit(solution)/shard_map/all_to_all | solution.py:117
  64.9 2.9 %collective-permute-start.7 = (f32[2,18,16,1]{3,2,1,0:T(8,128)S(1)}, f32[2,18,16,1]{3,2,1,0:T(8,128)S(1)}, u32[]{:S(2)}, u32[]{:S(2)}) collective-permute-start(f32[2,18,16,1]{3,2,1,0:T(8,128)S(1)} %get-tuple-element.9), channel_id=1, source_target_pairs={{1,0},{2,1},{3,2},{4,3},{5,4},{6,5},{7,6},{8,7},{9,8},{10,9},{11,1... | collective-permute-start | bytes 6920 | tf_op jit(solution)/shard_map/ppermute | solution.py:23
  68.3 4.0 %collective-permute-done.6 = f32[2,18,16,1]{3,2,1,0:T(8,128)S(1)} collective-permute-done((f32[2,18,16,1]{3,2,1,0:T(8,128)S(1)}, f32[2,18,16,1]{3,2,1,0:T(8,128)S(1)}, u32[]{:S(2)}, u32[]{:S(2)}) %collective-permute-start.6) | collective-permute-done | bytes 2336 | tf_op jit(solution)/shard_map/ppermute | solution.py:22
  72.6 1.3 gather_fusion.3
  73.9 1.3 gather_fusion.2
  75.3 1.3 gather_fusion.1
  78.0 1.6 fusion.91
  80.1 12.5 %all-to-all-start = ((f32[64,2,128]{2,1,0:T(2,128)}), f32[64,2,128]{2,1,0:T(2,128)S(1)}, u32[]{:S(2)}, u32[]{:S(2)}) async-start(f32[64,2,128]{2,1,0:T(2,128)} %fusion.91), calls=%async_computation | async-start | bytes 131072 | tf_op jit(solution)/shard_map/all_to_all | solution.py:118
  93.2 1.3 scatter_fusion.1
  94.5 3.5 %collective-permute-start.12 = (f32[2,1,16,128]{3,2,1,0:T(8,128)S(1)}, f32[2,1,16,128]{3,2,1,0:T(8,128)S(1)}, u32[]{:S(2)}, u32[]{:S(2)}) collective-permute-start(f32[2,1,16,128]{3,2,1,0:T(8,128)S(1)} %get-tuple-element.14), channel_id=1, source_target_pairs={{0,16},{16,32},{32,48},{48,64},{64,80},{80,96},{96,112},{112,128},... | collective-permute-start | bytes 49160 | tf_op jit(solution)/shard_map/ppermute | solution.py:22
  98.0 5.7 %collective-permute-start.13 = (f32[2,1,16,128]{3,2,1,0:T(8,128)S(1)}, f32[2,1,16,128]{3,2,1,0:T(8,128)S(1)}, u32[]{:S(2)}, u32[]{:S(2)}) collective-permute-start(f32[2,1,16,128]{3,2,1,0:T(8,128)S(1)} %get-tuple-element.15), channel_id=1, source_target_pairs={{16,0},{32,16},{48,32},{64,48},{80,64},{96,80},{112,96},{128,112},... | collective-permute-start | bytes 49160 | tf_op jit(solution)/shard_map/ppermute | solution.py:23
  106.5 2.6 %collective-permute-start.8 = (f32[1,16,128]{2,1,0:T(8,128)S(1)}, f32[1,16,128]{2,1,0:T(8,128)S(1)}, u32[]{:S(2)}, u32[]{:S(2)}) collective-permute-start(f32[1,16,128]{2,1,0:T(8,128)S(1)} %get-tuple-element.16), channel_id=1, source_target_pairs={{0,16},{16,32},{32,48},{48,64},{64,80},{80,96},{96,112},{112,128},... | collective-permute-start | bytes 24584 | tf_op jit(solution)/shard_map/ppermute | solution.py:22
  109.1 1.3 collective-permute-start.9
  110.6 2.9 %collective-permute-start.15 = (f32[2,18,16,1]{3,2,1,0:T(8,128)S(1)}, f32[2,18,16,1]{3,2,1,0:T(8,128)S(1)}, u32[]{:S(2)}, u32[]{:S(2)}) collective-permute-start(f32[2,18,16,1]{3,2,1,0:T(8,128)S(1)} %get-tuple-element.7), channel_id=1, source_target_pairs={{1,0},{2,1},{3,2},{4,3},{5,4},{6,5},{7,6},{8,7},{9,8},{10,9},{11,1... | collective-permute-start | bytes 6920 | tf_op jit(solution)/shard_map/ppermute | solution.py:23
  115.6 1.9 %collective-permute-start.10 = (f32[34,16,1]{2,1,0:T(8,128)}, f32[34,16,1]{2,1,0:T(8,128)S(1)}, u32[]{:S(2)}, u32[]{:S(2)}) collective-permute-start(f32[34,16,1]{2,1,0:T(8,128)} %get-tuple-element.10), channel_id=1, source_target_pairs={{0,1},{1,2},{2,3},{3,4},{4,5},{5,6},{6,7},{7,8},{8,9},{9,10},{10,1... | collective-permute-start | bytes 6536 | tf_op jit(solution)/shard_map/ppermute | solution.py:22
  117.5 5.1 %collective-permute-start.11 = (f32[34,16,1]{2,1,0:T(8,128)}, f32[34,16,1]{2,1,0:T(8,128)S(1)}, u32[]{:S(2)}, u32[]{:S(2)}) collective-permute-start(f32[34,16,1]{2,1,0:T(8,128)} %get-tuple-element.11), channel_id=1, source_target_pairs={{1,0},{2,1},{3,2},{4,3},{5,4},{6,5},{7,6},{8,7},{9,8},{10,9},{11,1... | collective-permute-start | bytes 6536 | tf_op jit(solution)/shard_map/ppermute | solution.py:23
  122.9 1.3 gather_fusion.11
  124.2 1.3 gather_fusion.10
  128.3 1.6 fusion.69
  130.0 12.0 %all-to-all-start.2 = ((f32[64,2,128]{2,1,0:T(2,128)}), f32[64,2,128]{2,1,0:T(2,128)S(1)}, u32[]{:S(2)}, u32[]{:S(2)}) async-start(f32[64,2,128]{2,1,0:T(2,128)} %fusion.69), calls=%async_computation.2 | async-start | bytes 131072 | tf_op jit(solution)/shard_map/all_to_all | solution.py:118
  148.2 1.6 fusion.58
  149.9 4.4 %all-to-all-done.2 = f32[64,2,128]{2,1,0:T(2,128)S(1)} async-done(((f32[64,2,128]{2,1,0:T(2,128)}), f32[64,2,128]{2,1,0:T(2,128)S(1)}, u32[]{:S(2)}, u32[]{:S(2)}) %all-to-all-start.2) | async-done | bytes 65568 | tf_op jit(solution)/shard_map/all_to_all | solution.py:118
  154.3 8.3 %all-to-all-start.3 = ((f32[64,2,128]{2,1,0:T(2,128)}), f32[64,2,128]{2,1,0:T(2,128)S(1)}, u32[]{:S(2)}, u32[]{:S(2)}) async-start(f32[64,2,128]{2,1,0:T(2,128)} %fusion.58), calls=%async_computation.3 | async-start | bytes 131072 | tf_op jit(solution)/shard_map/all_to_all | solution.py:117
  164.0 10.8 %all-to-all-done.3 = f32[64,2,128]{2,1,0:T(2,128)S(1)} async-done(((f32[64,2,128]{2,1,0:T(2,128)}), f32[64,2,128]{2,1,0:T(2,128)S(1)}, u32[]{:S(2)}, u32[]{:S(2)}) %all-to-all-start.3) | async-done | bytes 65568 | tf_op jit(solution)/shard_map/all_to_all | solution.py:117
  (126 shorter events, 39.5 us)
Async XLA Ops:
  0.6 36.4 %copy-start.3 = (f32[32,16,128]{2,1,0:T(8,128)S(1)}, f32[32,16,128]{2,1,0:T(8,128)}, u32[]{:S(2)}) copy-start(f32[32,16,128]{2,1,0:T(8,128)} %param.8) | copy-start | bytes 786436
  1.4 35.6 %collective-permute-start.1 = (f32[1,16,128]{2,1,0:T(8,128)S(1)}, f32[1,16,128]{2,1,0:T(8,128)S(1)}, u32[]{:S(2)}, u32[]{:S(2)}) collective-permute-start(f32[1,16,128]{2,1,0:T(8,128)S(1)} %get-tuple-element.20), channel_id=1, source_target_pairs={{16,0},{32,16},{48,32},{64,48},{80,64},{96,80},{112,96},{128,112},... | collective-permute-start | bytes 24584 | tf_op jit(solution)/shard_map/ppermute | solution.py:23
  2.7 34.3 %collective-permute-start = (f32[1,16,128]{2,1,0:T(8,128)S(1)}, f32[1,16,128]{2,1,0:T(8,128)S(1)}, u32[]{:S(2)}, u32[]{:S(2)}) collective-permute-start(f32[1,16,128]{2,1,0:T(8,128)S(1)} %get-tuple-element.21), channel_id=1, source_target_pairs={{0,16},{16,32},{32,48},{48,64},{64,80},{80,96},{96,112},{112,128},... | collective-permute-start | bytes 24584 | tf_op jit(solution)/shard_map/ppermute | solution.py:22
  8.0 56.7 %collective-permute-start.5 = (f32[2,1,16,128]{3,2,1,0:T(8,128)S(1)}, f32[2,1,16,128]{3,2,1,0:T(8,128)S(1)}, u32[]{:S(2)}, u32[]{:S(2)}) collective-permute-start(f32[2,1,16,128]{3,2,1,0:T(8,128)S(1)} %get-tuple-element.18), channel_id=1, source_target_pairs={{16,0},{32,16},{48,32},{64,48},{80,64},{96,80},{112,96},{128,112},... | collective-permute-start | bytes 49160 | tf_op jit(solution)/shard_map/ppermute | solution.py:23
  26.4 38.3 %collective-permute-start.4 = (f32[2,1,16,128]{3,2,1,0:T(8,128)S(1)}, f32[2,1,16,128]{3,2,1,0:T(8,128)S(1)}, u32[]{:S(2)}, u32[]{:S(2)}) collective-permute-start(f32[2,1,16,128]{3,2,1,0:T(8,128)S(1)} %get-tuple-element.19), channel_id=1, source_target_pairs={{0,16},{16,32},{32,48},{48,64},{64,80},{80,96},{96,112},{112,128},... | collective-permute-start | bytes 49160 | tf_op jit(solution)/shard_map/ppermute | solution.py:22
  37.2 9.8 %collective-permute-start.2 = (f32[34,16,1]{2,1,0:T(8,128)S(1)}, f32[34,16,1]{2,1,0:T(8,128)S(1)}, u32[]{:S(2)}, u32[]{:S(2)}) collective-permute-start(f32[34,16,1]{2,1,0:T(8,128)S(1)} %get-tuple-element.12), channel_id=1, source_target_pairs={{0,1},{1,2},{2,3},{3,4},{4,5},{5,6},{6,7},{7,8},{8,9},{9,10},{10,1... | collective-permute-start | bytes 6536 | tf_op jit(solution)/shard_map/ppermute | solution.py:22
  39.1 8.9 %collective-permute-start.3 = (f32[34,16,1]{2,1,0:T(8,128)S(1)}, f32[34,16,1]{2,1,0:T(8,128)S(1)}, u32[]{:S(2)}, u32[]{:S(2)}) collective-permute-start(f32[34,16,1]{2,1,0:T(8,128)S(1)} %get-tuple-element.13), channel_id=1, source_target_pairs={{1,0},{2,1},{3,2},{4,3},{5,4},{6,5},{7,6},{8,7},{9,8},{10,9},{11,1... | collective-permute-start | bytes 6536 | tf_op jit(solution)/shard_map/ppermute | solution.py:23
  53.8 10.9 %copy-start.2 = (f32[2,16,16,128]{3,2,1,0:T(8,128)S(1)}, f32[2,16,16,128]{3,2,1,0:T(8,128)}, u32[]{:S(2)}) copy-start(f32[2,16,16,128]{3,2,1,0:T(8,128)} %param.9) | copy-start | bytes 786436
  55.4 24.7 %all-to-all-start.1 = ((f32[64,2,128]{2,1,0:T(2,128)}), f32[64,2,128]{2,1,0:T(2,128)}, u32[]{:S(2)}, u32[]{:S(2)}) async-start(f32[64,2,128]{2,1,0:T(2,128)} %fusion.80), calls=%async_computation.1 | async-start | bytes 131072 | tf_op jit(solution)/shard_map/all_to_all | solution.py:117
  64.9 7.4 %collective-permute-start.6 = (f32[2,18,16,1]{3,2,1,0:T(8,128)S(1)}, f32[2,18,16,1]{3,2,1,0:T(8,128)S(1)}, u32[]{:S(2)}, u32[]{:S(2)}) collective-permute-start(f32[2,18,16,1]{3,2,1,0:T(8,128)S(1)} %get-tuple-element.8), channel_id=1, source_target_pairs={{0,1},{1,2},{2,3},{3,4},{4,5},{5,6},{6,7},{7,8},{8,9},{9,10},{10,1... | collective-permute-start | bytes 6920 | tf_op jit(solution)/shard_map/ppermute | solution.py:22
  64.9 7.3 %collective-permute-start.7 = (f32[2,18,16,1]{3,2,1,0:T(8,128)S(1)}, f32[2,18,16,1]{3,2,1,0:T(8,128)S(1)}, u32[]{:S(2)}, u32[]{:S(2)}) collective-permute-start(f32[2,18,16,1]{3,2,1,0:T(8,128)S(1)} %get-tuple-element.9), channel_id=1, source_target_pairs={{1,0},{2,1},{3,2},{4,3},{5,4},{6,5},{7,6},{8,7},{9,8},{10,9},{11,1... | collective-permute-start | bytes 6920 | tf_op jit(solution)/shard_map/ppermute | solution.py:23
  80.1 24.7 %all-to-all-start = ((f32[64,2,128]{2,1,0:T(2,128)}), f32[64,2,128]{2,1,0:T(2,128)S(1)}, u32[]{:S(2)}, u32[]{:S(2)}) async-start(f32[64,2,128]{2,1,0:T(2,128)} %fusion.91), calls=%async_computation | async-start | bytes 131072 | tf_op jit(solution)/shard_map/all_to_all | solution.py:118
  92.6 0.6 copy-start.4
  94.5 15.9 %collective-permute-start.12 = (f32[2,1,16,128]{3,2,1,0:T(8,128)S(1)}, f32[2,1,16,128]{3,2,1,0:T(8,128)S(1)}, u32[]{:S(2)}, u32[]{:S(2)}) collective-permute-start(f32[2,1,16,128]{3,2,1,0:T(8,128)S(1)} %get-tuple-element.14), channel_id=1, source_target_pairs={{0,16},{16,32},{32,48},{48,64},{64,80},{80,96},{96,112},{112,128},... | collective-permute-start | bytes 49160 | tf_op jit(solution)/shard_map/ppermute | solution.py:22
  98.0 12.4 %collective-permute-start.13 = (f32[2,1,16,128]{3,2,1,0:T(8,128)S(1)}, f32[2,1,16,128]{3,2,1,0:T(8,128)S(1)}, u32[]{:S(2)}, u32[]{:S(2)}) collective-permute-start(f32[2,1,16,128]{3,2,1,0:T(8,128)S(1)} %get-tuple-element.15), channel_id=1, source_target_pairs={{16,0},{32,16},{48,32},{64,48},{80,64},{96,80},{112,96},{128,112},... | collective-permute-start | bytes 49160 | tf_op jit(solution)/shard_map/ppermute | solution.py:23
  104.8 0.7 copy-start.5
  106.5 7.1 %collective-permute-start.8 = (f32[1,16,128]{2,1,0:T(8,128)S(1)}, f32[1,16,128]{2,1,0:T(8,128)S(1)}, u32[]{:S(2)}, u32[]{:S(2)}) collective-permute-start(f32[1,16,128]{2,1,0:T(8,128)S(1)} %get-tuple-element.16), channel_id=1, source_target_pairs={{0,16},{16,32},{32,48},{48,64},{64,80},{80,96},{96,112},{112,128},... | collective-permute-start | bytes 24584 | tf_op jit(solution)/shard_map/ppermute | solution.py:22
  109.1 5.5 %collective-permute-start.9 = (f32[1,16,128]{2,1,0:T(8,128)S(1)}, f32[1,16,128]{2,1,0:T(8,128)S(1)}, u32[]{:S(2)}, u32[]{:S(2)}) collective-permute-start(f32[1,16,128]{2,1,0:T(8,128)S(1)} %get-tuple-element.17), channel_id=1, source_target_pairs={{16,0},{32,16},{48,32},{64,48},{80,64},{96,80},{112,96},{128,112},... | collective-permute-start | bytes 24584 | tf_op jit(solution)/shard_map/ppermute | solution.py:23
  110.6 12.0 %collective-permute-start.14 = (f32[2,18,16,1]{3,2,1,0:T(8,128)S(1)}, f32[2,18,16,1]{3,2,1,0:T(8,128)S(1)}, u32[]{:S(2)}, u32[]{:S(2)}) collective-permute-start(f32[2,18,16,1]{3,2,1,0:T(8,128)S(1)} %get-tuple-element.6), channel_id=1, source_target_pairs={{0,1},{1,2},{2,3},{3,4},{4,5},{5,6},{6,7},{7,8},{8,9},{9,10},{10,1... | collective-permute-start | bytes 6920 | tf_op jit(solution)/shard_map/ppermute | solution.py:22
  110.6 11.9 %collective-permute-start.15 = (f32[2,18,16,1]{3,2,1,0:T(8,128)S(1)}, f32[2,18,16,1]{3,2,1,0:T(8,128)S(1)}, u32[]{:S(2)}, u32[]{:S(2)}) collective-permute-start(f32[2,18,16,1]{3,2,1,0:T(8,128)S(1)} %get-tuple-element.7), channel_id=1, source_target_pairs={{1,0},{2,1},{3,2},{4,3},{5,4},{6,5},{7,6},{8,7},{9,8},{10,9},{11,1... | collective-permute-start | bytes 6920 | tf_op jit(solution)/shard_map/ppermute | solution.py:23
  115.6 26.9 %collective-permute-start.10 = (f32[34,16,1]{2,1,0:T(8,128)}, f32[34,16,1]{2,1,0:T(8,128)S(1)}, u32[]{:S(2)}, u32[]{:S(2)}) collective-permute-start(f32[34,16,1]{2,1,0:T(8,128)} %get-tuple-element.10), channel_id=1, source_target_pairs={{0,1},{1,2},{2,3},{3,4},{4,5},{5,6},{6,7},{7,8},{8,9},{9,10},{10,1... | collective-permute-start | bytes 6536 | tf_op jit(solution)/shard_map/ppermute | solution.py:22
  117.5 25.0 %collective-permute-start.11 = (f32[34,16,1]{2,1,0:T(8,128)}, f32[34,16,1]{2,1,0:T(8,128)S(1)}, u32[]{:S(2)}, u32[]{:S(2)}) collective-permute-start(f32[34,16,1]{2,1,0:T(8,128)} %get-tuple-element.11), channel_id=1, source_target_pairs={{1,0},{2,1},{3,2},{4,3},{5,4},{6,5},{7,6},{8,7},{9,8},{10,9},{11,1... | collective-permute-start | bytes 6536 | tf_op jit(solution)/shard_map/ppermute | solution.py:23
  130.0 24.3 %all-to-all-start.2 = ((f32[64,2,128]{2,1,0:T(2,128)}), f32[64,2,128]{2,1,0:T(2,128)S(1)}, u32[]{:S(2)}, u32[]{:S(2)}) async-start(f32[64,2,128]{2,1,0:T(2,128)} %fusion.69), calls=%async_computation.2 | async-start | bytes 131072 | tf_op jit(solution)/shard_map/all_to_all | solution.py:118
  154.3 20.5 %all-to-all-start.3 = ((f32[64,2,128]{2,1,0:T(2,128)}), f32[64,2,128]{2,1,0:T(2,128)S(1)}, u32[]{:S(2)}, u32[]{:S(2)}) async-start(f32[64,2,128]{2,1,0:T(2,128)} %fusion.58), calls=%async_computation.3 | async-start | bytes 131072 | tf_op jit(solution)/shard_map/all_to_all | solution.py:117
  164.0 11.8 %copy-start = (f32[512,128]{1,0:T(8,128)}, f32[512,128]{1,0:T(8,128)S(1)}, u32[]{:S(2)}) copy-start(f32[512,128]{1,0:T(8,128)S(1)} %scatter_fusion.2) | copy-start | bytes 786436
  175.8 0.7 copy-start.1
where the time goes:
time: 177 us
  starting transfers between devices  101 us (57%)
  local copies, waits for them, and re-layouts  37 us (21%)
  waiting for transfers between devices  22.4 us (13%)
  other arithmetic  14.8 us (8%)
    ppermute x8, starting transfers between devices, extended(): after = lax.ppermute(initial, axis, down)  42.5 us
    all_to_all x2, starting transfers between devices, per_device(): lax.all_to_all(return_values, 'gx', split_axis=0, concat_axis=0, tiled=True)  24.5 us
    gather x32, local copies, waits for them, and re-layouts, trilinear(): picked = field[first_row + shift_a, second_row + shift_b]  21.7 us
    all_to_all x2, starting transfers between devices, per_device(): lax.all_to_all(donor_values, 'gx', split_axis=0, concat_axis=0, tiled=True)  17.6 us
    ppermute x8, starting transfers between devices, extended(): before = lax.ppermute(last, axis, up)  16.4 us
    all_to_all x2, waiting for transfers between devices, per_device(): lax.all_to_all(donor_values, 'gx', split_axis=0, concat_axis=0, tiled=True)  10.8 us
    add x4, other arithmetic, trilinear(): blended = portion if blended is None else blended + portion  6.58 us
    all_to_all x2, waiting for transfers between devices, per_device(): lax.all_to_all(return_values, 'gx', split_axis=0, concat_axis=0, tiled=True)  5.5 us
  transfers between devices with their start and end apart: 20, of which 6 were waited for; matrix products, arithmetic and copies ran while one was open for 27% of the time, Pallas kernels for 0%

commit v1 on v0

v1 whole, which is shorter than its diff:
```python
import functools

import jax
import jax.numpy as jnp
from jax import lax
from jax.experimental import pallas as pl
from jax.experimental.pallas import tpu as pltpu
from jax.sharding import PartitionSpec as P

STEPS = 2
MESH = pl.DeviceIdType.MESH

BACK = (0.3, 0.25, 0.15, 0.04)
BODY = (0.2, 0.3, 0.2, 0.045)

GROUPS = ((1, 32, 0), (35, 16, 32), (53, 16, 48))
PLANES = 70
Z = 16
LANES = 128
F32 = jnp.float32
BF16 = jnp.bfloat16


def iota(shape, dim):
    return lax.broadcasted_iota(jnp.int32, shape, dim)


def split(value):
    high = value.astype(BF16)
    return high, (value - high.astype(F32)).astype(BF16)


def dot(a, b):
    return jnp.dot(a, b, preferred_element_type=F32)


def exact_dot(a, b, dims=((1,), (0,))):
    return lax.dot_general(
        a, b, (dims, ((), ())), precision=lax.Precision.HIGHEST, preferred_element_type=F32
    )


def kernel(
    nx,
    ny,
    back_ref,
    body_ref,
    donor_rows,
    donor_fractions,
    fringe_slots,
    return_rows,
    return_fractions,
    hole_slots,
    back_out,
    body_out,
    field,
    moved,
    table,
    w_high,
    w_low,
    w_halo,
    w_x,
    w_z,
    share_y,
    place,
    keep,
    edge,
    edge_above,
    edge_below,
    edge_corner,
    sent,
    got,
    in_sem,
    halo_send,
    halo_recv,
    swap_send,
    swap_recv,
    out_sem,
):
    q = lax.axis_index("gx")
    j = lax.axis_index("gy")
    q_up, q_down = lax.rem(q + 1, nx), lax.rem(q + nx - 1, nx)
    j_up, j_down = lax.rem(j + 1, ny), lax.rem(j + ny - 1, ny)

    loads = [
        pltpu.make_async_copy(back_ref, field.at[0, pl.ds(1, 32)], in_sem.at[0]),
        pltpu.make_async_copy(body_ref.at[0], field.at[0, pl.ds(35, 16)], in_sem.at[1]),
        pltpu.make_async_copy(body_ref.at[1], field.at[0, pl.ds(53, 16)], in_sem.at[2]),
    ]
    for load in loads:
        load.start()

    barrier = pltpu.get_barrier_semaphore()

    def greet(step, carry):
        pl.semaphore_signal(
            barrier, inc=1, device_id={"gx": lax.rem(q + step, nx)}, device_id_type=MESH
        )
        return carry

    lax.fori_loop(1, nx, greet, 0)
    for there in ((q, j_up), (q, j_down), (q_down, j_down), (q_up, j_up)):
        pl.semaphore_signal(
            barrier, inc=1, device_id={"gx": there[0], "gy": there[1]}, device_id_type=MESH
        )

    def halo_copies(now):
        f = field.at[now]
        pairs = []
        for n, (first, count, _) in enumerate(GROUPS):
            pairs.append((f.at[first + count - 1], f.at[first - 1], q_up, j))
            pairs.append((f.at[first], f.at[first + count], q_down, j))
        pairs.append((edge.at[now], edge_below.at[now], q, j_up))
        pairs.append((edge.at[now], edge_above.at[now], q, j_down))
        pairs.append((edge.at[now], edge_corner.at[now], q_down, j_down))
        return [
            pltpu.make_async_remote_copy(
                src_ref=src,
                dst_ref=dst,
                send_sem=halo_send.at[now, n],
                recv_sem=halo_recv.at[now, n],
                device_id={"gx": to_q, "gy": to_j},
                device_id_type=MESH,
            )
            for n, (src, dst, to_q, to_j) in enumerate(pairs)
        ]

    lane = iota((Z, LANES), 1)

    def pack_edges(now):
        packed = jnp.zeros((Z, LANES), F32)
        for first, count, plane in GROUPS:
            for k in range(count):
                spot = 2 * (plane + k)
                rolled = pltpu.roll(field[now, first + k], spot, 1)
                hit = (lane == spot) | (lane == (spot - 1) % LANES)
                packed = jnp.where(hit, rolled, packed)
        edge[now] = packed

    for load in loads:
        load.wait()
    pack_edges(0)
    pl.semaphore_wait(barrier, nx - 1 + 4)
    for copy in halo_copies(0):
        copy.start()

    table[...] = jnp.zeros_like(table)
    half = ((donor_rows, return_rows), (fringe_slots, hole_slots))
    for n, (first, second) in enumerate(half):
        table[4 * n : 4 * n + 2, 0:64] = first[...].astype(F32)
        table[4 * n + 2 : 4 * n + 4, 0:64] = second[...].astype(F32)
    for n in range(3):
        table[8 + 4 * n : 10 + 4 * n, 0:64] = donor_fractions[n]
        table[10 + 4 * n : 12 + 4 * n, 0:64] = return_fractions[n]
    rows = 4 * 64
    spread = (iota((LANES, rows), 1) // 4 == iota((LANES, rows), 0)).astype(F32)
    wide = exact_dot(table[...], spread)
    kind = iota((1, rows), 1) % 4

    def pick(n):
        x = wide[4 * n : 4 * n + 4]
        return jnp.where(
            kind == 0, x[0:1], jnp.where(kind == 1, x[1:2], jnp.where(kind == 2, x[2:3], x[3:4]))
        )

    row = jnp.maximum(pick(0), 0.0)
    slot = pick(1)
    donor = kind < 2
    used = jnp.where(donor, float(Z - 1), float(Z - 3))
    plane = jnp.floor((row + 0.5) / used)
    layer = row - plane * used
    plane = jnp.where(donor, plane, plane + 32.0)
    target = jnp.where(slot < 0.0, -1.0, jnp.where(donor, slot + 512.0, slot))
    columns = jnp.concatenate(
        [plane, layer, pick(2), pick(3), pick(4), jnp.zeros((3, rows), F32)], axis=0
    ).T
    plane_c = columns[:, 0:1].astype(jnp.int32)
    layer_c = columns[:, 1:2].astype(jnp.int32)
    f1, f2, f3 = columns[:, 2:3], columns[:, 3:4], columns[:, 4:5]
    share_y[...] = jnp.broadcast_to(f3, (rows, LANES))
    last = (plane_c == 31) | (plane_c == 47) | (plane_c == 63)
    halo_index = jnp.where(plane_c == 31, 0, jnp.where(plane_c == 47, 1, 2))
    w00, w01 = (1.0 - f1) * (1.0 - f2), (1.0 - f1) * f2
    w10, w11 = f1 * (1.0 - f2), f1 * f2
    base = plane_c * Z + layer_c
    far = jnp.where(last, -1000, base + Z)

    def weigh(n, carry):
        k = iota((rows, LANES), 1) + n * LANES
        w = (
            jnp.where(k == base, w00, 0.0)
            + jnp.where(k == base + 1, w01, 0.0)
            + jnp.where(k == far, w10, 0.0)
            + jnp.where(k == far + 1, w11, 0.0)
        )
        high, low = split(w)
        w_high[n] = high
        w_low[n] = low
        return carry

    lax.fori_loop(0, 8, weigh, 0)
    k = iota((rows, LANES), 1)
    near = jnp.where(last, halo_index * Z + layer_c, -1000)
    w_halo[...] = jnp.where(k == near, w10, 0.0) + jnp.where(k == near + 1, w11, 0.0)
    beyond = jnp.where(last, 1 + 2 * halo_index, 2 * plane_c + 2)
    w_x[...] = jnp.where(k == 2 * plane_c, 1.0 - f1, 0.0) + jnp.where(k == beyond, f1, 0.0)
    w_z[...] = jnp.where(k == layer_c, 1.0 - f2, 0.0) + jnp.where(k == layer_c + 1, f2, 0.0)

    target_i = target.astype(jnp.int32)
    ones = jnp.ones((rows, LANES), BF16)

    def lay_back(n, carry):
        r = iota((LANES, rows), 0) + n * LANES
        hit = jnp.where(r == target_i, 1.0, 0.0).astype(BF16)
        place[n] = hit
        keep[n] = 1.0 - dot(hit, ones)
        return carry

    lax.fori_loop(0, 4, lay_back, 0)

    def lay_body(n, carry):
        r = iota((LANES, rows), 0)
        r = 512 + (r // 8 + n * 16) * Z + 8 + r % 8
        place[4 + n] = jnp.where(r == target_i, 1.0, 0.0).astype(BF16)
        return carry

    lax.fori_loop(0, 2, lay_body, 0)

    for now in range(STEPS):
        final = now == STEPS - 1
        f = field.at[now]

        blend = jnp.zeros((rows, LANES), F32)
        for first, count, plane in GROUPS:
            for part in range(count // 8):
                high, low = split(f[first + 8 * part : first + 8 * part + 8].reshape(LANES, LANES))
                n = plane // 8 + part
                both = dot(w_high[n], jnp.concatenate([high, low], axis=1))
                blend += both[:, :LANES] + both[:, LANES:] + dot(w_low[n], high)

        for copy in halo_copies(now):
            copy.wait_recv()

        zero = jnp.zeros((Z, LANES), F32)
        f[0] = jnp.where(q == 0, zero, f[0])
        f[33] = jnp.where(q == nx - 1, zero, f[33])
        in_back = lane < 63
        below = jnp.where((j == 0) & (in_back | (lane == 127)), zero, edge_below[now])
        above = jnp.where((j == ny - 1) & in_back, zero, edge_above[now])
        even = lane % 2 == 0
        edges = jnp.where(even, above, below)
        corner = edge_corner[now]
        corner_back = jnp.where((j == ny - 1) | (q == nx - 1), zero, corner)
        high_y = jnp.where(even, above, zero)
        high_y = jnp.where(lane == 1, pltpu.roll(corner_back, 1, 1), high_y)
        high_y = jnp.where(lane == 3, pltpu.roll(corner, LANES - 61, 1), high_y)
        high_y = jnp.where(lane == 5, pltpu.roll(corner, LANES - 91, 1), high_y)

        beyond_x = jnp.concatenate([f[33], f[51], f[69]], axis=0)
        blend += exact_dot(w_halo[:, 0:48], beyond_x)
        high_y = jnp.concatenate([high_y, jnp.zeros((LANES - Z, LANES), F32)], axis=0)
        spill = exact_dot(w_x[...], high_y, ((1,), (1,)))
        spill = jnp.sum(w_z[...] * spill, axis=1, keepdims=True)
        ahead = pltpu.roll(blend, LANES - 1, 1)
        ahead = jnp.where(iota((rows, LANES), 1) == LANES - 1, spill, ahead)
        mixed = blend + share_y[...] * (ahead - blend)
        sent[now] = mixed.reshape(64, 4, LANES)

        def send(step, carry):
            to = lax.rem(q + step, nx)
            pltpu.make_async_remote_copy(
                src_ref=sent.at[now, to],
                dst_ref=got.at[now, q],
                send_sem=swap_send.at[now],
                recv_sem=swap_recv.at[now],
                device_id={"gx": to},
                device_id_type=MESH,
            ).start()
            return carry

        lax.fori_loop(1, nx, send, 0)
        got[now, pl.ds(q, 1)] = sent[now, pl.ds(q, 1)]

        for first, count, plane in GROUPS:
            a, b, c, d = BACK if count == 32 else BODY
            layers = iota((Z, LANES), 0)

            def step_plane(n, carry, first=first, plane=plane, a=a, b=b, c=c, d=d):
                here = f[first + n]
                side = pltpu.roll(edges, LANES - 2 * (plane + n), 1)
                back_y = pltpu.roll(jnp.where(lane == LANES - 1, side, here), 1, 1)
                ahead_y = pltpu.roll(jnp.where(lane == 0, side, here), LANES - 1, 1)
                back_z = jnp.where(layers == 0, 0.0, pltpu.roll(here, 1, 0))
                ahead_z = jnp.where(layers == Z - 1, 0.0, pltpu.roll(here, Z - 1, 0))
                new = (
                    (1.0 - a - b - c - 6.0 * d) * here
                    + (a + d) * f[first + n - 1]
                    + d * f[first + n + 1]
                    + (b + d) * back_y
                    + d * ahead_y
                    + (c + d) * back_z
                    + d * ahead_z
                )
                if plane == 0:
                    new = new * keep[n // 8, pl.ds(pl.multiple_of(n % 8 * Z, Z), Z)]
                else:
                    new = jnp.where(layers >= Z - 2, 0.0, new)
                moved[plane + n] = new
                return carry

            for n in range(count):
                step_plane(n, 0)

        pltpu.make_async_remote_copy(
            src_ref=sent.at[now, pl.ds(0, nx - 1)],
            dst_ref=got.at[now, pl.ds(0, nx - 1)],
            send_sem=swap_send.at[now],
            recv_sem=swap_recv.at[now],
            device_id={"gx": q_up},
            device_id_type=MESH,
        ).wait_recv()

        high, low = split(got[now].reshape(rows, LANES))
        received = jnp.concatenate([high, low], axis=1)
        for n in range(6):
            both = dot(place[n], received)
            added = both[:, :LANES] + both[:, LANES:]
            if n < 4:
                new = moved[8 * n : 8 * n + 8] + added.reshape(8, Z, LANES)
                if final:
                    back_out[8 * n : 8 * n + 8] = new
                else:
                    field[now + 1, 1 + 8 * n : 9 + 8 * n] = new
            else:
                start = 32 + 16 * (n - 4)
                low_part = moved[start : start + 16, 0:8]
                new = moved[start : start + 16, 8:16] + added.reshape(16, 8, LANES)
                if final:
                    body_out[n - 4, :, 0:8] = low_part
                    body_out[n - 4, :, 8:16] = new
                else:
                    first = GROUPS[n - 3][0]
                    field[now + 1, first : first + 16, 0:8] = low_part
                    field[now + 1, first : first + 16, 8:16] = new
        if not final:
            pack_edges(now + 1)
            for copy in halo_copies(now + 1):
                copy.start()

    for now in range(STEPS):
        for copy in halo_copies(now):
            copy.wait_send()
        pltpu.make_async_remote_copy(
            src_ref=sent.at[now, pl.ds(0, nx - 1)],
            dst_ref=got.at[now, pl.ds(0, nx - 1)],
            send_sem=swap_send.at[now],
            recv_sem=swap_recv.at[now],
            device_id={"gx": q_up},
            device_id_type=MESH,
        ).wait_send()


def per_device(
    background,
    nearbody,
    donor_rows,
    donor_fractions,
    fringe_slots,
    return_rows,
    return_fractions,
    hole_slots,
):
    nx, ny = lax.axis_size("gx"), lax.axis_size("gy")
    by_slot = lambda rows: jnp.swapaxes(rows[0, 0], 0, 1)
    shares = lambda parts: jnp.swapaxes(parts[:, 0, 0], 1, 2)
    vmem = pl.BlockSpec(memory_space=pltpu.VMEM)
    hbm = pl.BlockSpec(memory_space=pl.ANY)
    dma = pltpu.SemaphoreType.DMA
    return pl.pallas_call(
        functools.partial(kernel, nx, ny),
        out_shape=(
            jax.ShapeDtypeStruct(background.shape, F32),
            jax.ShapeDtypeStruct(nearbody.shape, F32),
        ),
        in_specs=[hbm, hbm] + [vmem] * 6,
        out_specs=(vmem, vmem),
        scratch_shapes=[
            pltpu.VMEM((STEPS, PLANES, Z, LANES), F32),
            pltpu.VMEM((64, Z, LANES), F32),
            pltpu.VMEM((24, LANES), F32),
            pltpu.VMEM((8, 256, LANES), BF16),
            pltpu.VMEM((8, 256, LANES), BF16),
            pltpu.VMEM((256, LANES), F32),
            pltpu.VMEM((256, LANES), F32),
            pltpu.VMEM((256, LANES), F32),
            pltpu.VMEM((256, LANES), F32),
            pltpu.VMEM((6, LANES, 256), BF16),
            pltpu.VMEM((4, LANES, LANES), F32),
            pltpu.VMEM((STEPS, Z, LANES), F32),
            pltpu.VMEM((STEPS, Z, LANES), F32),
            pltpu.VMEM((STEPS, Z, LANES), F32),
            pltpu.VMEM((STEPS, Z, LANES), F32),
            pltpu.VMEM((STEPS, 64, 4, LANES), F32),
            pltpu.VMEM((STEPS, 64, 4, LANES), F32),
            dma((3,)),
            dma((STEPS, 9)),
            dma((STEPS, 9)),
            dma((STEPS,)),
            dma((STEPS,)),
            dma((3,)),
        ],
        compiler_params=pltpu.CompilerParams(
            collective_id=0, has_side_effects=True, vmem_limit_bytes=32 * 1024 * 1024
        ),
        name="overset_steps",
    )(
        background,
        nearbody,
        by_slot(donor_rows),
        shares(donor_fractions),
        by_slot(fringe_slots),
        by_slot(return_rows),
        shares(return_fractions),
        by_slot(hole_slots),
    )


def solution(mesh):
    placed = (
        P("gx", None, "gy"),
        P(None, "gx", None, "gy"),
        P("gx", "gy", None, None),
        P(None, "gx", "gy", None, None),
        P("gx", "gy", None, None),
        P("gx", "gy", None, None),
        P(None, "gx", "gy", None, None),
        P("gx", "gy", None, None),
    )
    return jax.shard_map(
        per_device,
        mesh=mesh,
        in_specs=placed,
        out_specs=(P("gx", None, "gy"), P(None, "gx", None, "gy")),
        check_vma=False,
    )
```

time: 177 us -> 53.4 us (0.30)
  the two profiles are of different devices: /device:TPU:64 before, /device:TPU:1 now
where the time goes in v1:
time: 53.4 us; the launch traced here: 53.1 us
  Pallas kernels  48.4 us (91%)
  local copies, waits for them, and re-layouts  4.02 us (8%)
  between operations  0.69 us (1%)
    pallas_call x1, Pallas kernels, per_device(): pl.pallas_call(functools.partial(kernel, nx, ny), out_shape=(jax.ShapeDty...  48.4 us
    unnamed x18, local copies, waits for them, and re-layouts  4.02 us

profile of v1, /device:TPU:1, one launch (start us, length us, event | category | flops | bytes accessed | tf_op | source)
XLA Modules:
  0.0 53.1 jit_solution(548098872694695492)
XLA Ops:
  0.6 0.0 copy-start.7
  0.6 0.0 copy-start.5
  0.7 0.0 copy-start.6
  0.7 0.0 copy-start.3
  0.7 0.0 copy-start.2
  0.7 0.0 copy-start.4
  0.7 0.6 %copy-done.7 = s32[1,1,64,2]{2,3,1,0:T(2,128)S(1)} copy-done((s32[1,1,64,2]{2,3,1,0:T(2,128)S(1)}, s32[1,1,64,2]{2,3,1,0:T(2,128)}, u32[]{:S(2)}) %copy-start.7) | copy-done | bytes 536
  1.3 0.0 copy-done.5
  1.3 0.0 copy-done.6
  1.3 0.0 copy-done.3
  1.4 0.0 copy-done.2
  1.4 0.0 copy-done.4
  1.4 0.0 copy-start
  1.4 0.9 %copy-done = f32[32,16,128]{2,1,0:T(8,128)S(1)} copy-done((f32[32,16,128]{2,1,0:T(8,128)S(1)}, f32[32,16,128]{2,1,0:T(8,128)}, u32[]{:S(2)}) %copy-start) | copy-done | bytes 262168
  2.3 0.0 copy-start.1
  2.3 0.9 %copy-done.1 = f32[2,16,16,128]{3,2,1,0:T(8,128)S(1)} copy-done((f32[2,16,16,128]{3,2,1,0:T(8,128)S(1)}, f32[2,16,16,128]{3,2,1,0:T(8,128)}, u32[]{:S(2)}) %copy-start.1) | copy-done | bytes 262168
  3.3 48.4 %overset_steps.1 = (f32[32,16,128]{2,1,0:T(8,128)S(1)}, f32[2,16,16,128]{3,2,1,0:T(8,128)S(1)}) custom-call(f32[32,16,128]{2,1,0:T(8,128)S(1)} %copy-done, f32[2,16,16,128]{3,2,1,0:T(8,128)S(1)} %copy-done.1, s32[2,64]{1,0:T(2,128)S(1)} %bitcast.20, f32[3,2,64]{2,1,0:T(2,128)S(1)} %bitcast.18, s32[2,64]{1,0:T(2,128)S(1)} %bitcast.21, s32[2,64]{1,0:T(2,128)S(1)} %bitcast.22, ...), custom_call_target="tpu_custom_call" | custom-call | tf_op jit(solution)/shard_map/overset_steps/pallas_call | solution.py:379
  51.7 0.7 %copy.12 = f32[32,16,128]{2,1,0:T(8,128)} copy(f32[32,16,128]{2,1,0:T(8,128)S(1)} %get-tuple-element.4) | data formatting | bytes 524288
  52.4 0.7 %copy.13 = f32[2,16,16,128]{3,2,1,0:T(8,128)} copy(f32[2,16,16,128]{3,2,1,0:T(8,128)S(1)} %get-tuple-element.5) | data formatting | bytes 524288
Async XLA Ops:
  0.6 0.7 %copy-start.7 = (s32[1,1,64,2]{2,3,1,0:T(2,128)S(1)}, s32[1,1,64,2]{2,3,1,0:T(2,128)}, u32[]{:S(2)}) copy-start(s32[1,1,64,2]{2,3,1,0:T(2,128)} %param.15) | copy-start | bytes 1540
  0.6 0.7 %copy-start.5 = (s32[1,1,64,2]{2,3,1,0:T(2,128)S(1)}, s32[1,1,64,2]{2,3,1,0:T(2,128)}, u32[]{:S(2)}) copy-start(s32[1,1,64,2]{2,3,1,0:T(2,128)} %param.12) | copy-start | bytes 1540
  0.7 0.7 %copy-start.6 = (s32[1,1,64,2]{2,3,1,0:T(2,128)S(1)}, s32[1,1,64,2]{2,3,1,0:T(2,128)}, u32[]{:S(2)}) copy-start(s32[1,1,64,2]{2,3,1,0:T(2,128)} %param.13) | copy-start | bytes 1540
  0.7 0.7 %copy-start.3 = (f32[3,1,1,64,2]{3,4,2,1,0:T(2,128)S(1)}, f32[3,1,1,64,2]{3,4,2,1,0:T(2,128)}, u32[]{:S(2)}) copy-start(f32[3,1,1,64,2]{3,4,2,1,0:T(2,128)} %param.14) | copy-start | bytes 4612
  0.7 0.7 %copy-start.2 = (f32[3,1,1,64,2]{3,4,2,1,0:T(2,128)S(1)}, f32[3,1,1,64,2]{3,4,2,1,0:T(2,128)}, u32[]{:S(2)}) copy-start(f32[3,1,1,64,2]{3,4,2,1,0:T(2,128)} %param.11) | copy-start | bytes 4612
  0.7 0.7 %copy-start.4 = (s32[1,1,64,2]{2,3,1,0:T(2,128)S(1)}, s32[1,1,64,2]{2,3,1,0:T(2,128)}, u32[]{:S(2)}) copy-start(s32[1,1,64,2]{2,3,1,0:T(2,128)} %param.10) | copy-start | bytes 1540
  1.4 0.9 %copy-start = (f32[32,16,128]{2,1,0:T(8,128)S(1)}, f32[32,16,128]{2,1,0:T(8,128)}, u32[]{:S(2)}) copy-start(f32[32,16,128]{2,1,0:T(8,128)} %back_ref.1) | copy-start | bytes 786436
  2.3 0.9 %copy-start.1 = (f32[2,16,16,128]{3,2,1,0:T(8,128)S(1)}, f32[2,16,16,128]{3,2,1,0:T(8,128)}, u32[]{:S(2)}) copy-start(f32[2,16,16,128]{3,2,1,0:T(8,128)} %body_ref.1) | copy-start | bytes 786436

commit v2 on v1

--- a/solution.py
+++ b/solution.py
@@ -40,19 +40,32 @@
     )
 
 
+def peer(q, step):
+    def away(n):
+        return 4 + (1 - 2 * (n % 2)) * ((n + 1) // 2)
+
+    return (q // 8 + away(step // 8)) % 8 * 8 + (q % 8 + away(step % 8)) % 8
+
+
 def kernel(
     nx,
     ny,
     back_ref,
     body_ref,
+    donor_rows_ref,
+    donor_fractions_ref,
+    fringe_slots_ref,
+    return_rows_ref,
+    return_fractions_ref,
+    hole_slots_ref,
+    back_out,
+    body_out,
     donor_rows,
     donor_fractions,
     fringe_slots,
     return_rows,
     return_fractions,
     hole_slots,
-    back_out,
-    body_out,
     field,
     moved,
     table,
@@ -75,7 +88,6 @@
     halo_recv,
     swap_send,
     swap_recv,
-    out_sem,
 ):
     q = lax.axis_index("gx")
     j = lax.axis_index("gy")
@@ -87,18 +99,29 @@
         pltpu.make_async_copy(body_ref.at[0], field.at[0, pl.ds(35, 16)], in_sem.at[1]),
         pltpu.make_async_copy(body_ref.at[1], field.at[0, pl.ds(53, 16)], in_sem.at[2]),
     ]
-    for load in loads:
+    tables = [
+        pltpu.make_async_copy(src, dst, in_sem.at[3 + n])
+        for n, (src, dst) in enumerate(
+            (
+                (donor_rows_ref, donor_rows),
+                (donor_fractions_ref, donor_fractions),
+                (fringe_slots_ref, fringe_slots),
+                (return_rows_ref, return_rows),
+                (return_fractions_ref, return_fractions),
+                (hole_slots_ref, hole_slots),
+            )
+        )
+    ]
+    for load in loads + tables:
         load.start()
 
     barrier = pltpu.get_barrier_semaphore()
 
     def greet(step, carry):
-        pl.semaphore_signal(
-            barrier, inc=1, device_id={"gx": lax.rem(q + step, nx)}, device_id_type=MESH
-        )
+        pl.semaphore_signal(barrier, inc=1, device_id={"gx": peer(q, step)}, device_id_type=MESH)
         return carry
 
-    lax.fori_loop(1, nx, greet, 0)
+    lax.fori_loop(0, nx - 1, greet, 0, unroll=True)
     for there in ((q, j_up), (q, j_down), (q_down, j_down), (q_up, j_up)):
         pl.semaphore_signal(
             barrier, inc=1, device_id={"gx": there[0], "gy": there[1]}, device_id_type=MESH
@@ -137,13 +160,8 @@
                 packed = jnp.where(hit, rolled, packed)
         edge[now] = packed
 
-    for load in loads:
+    for load in tables:
         load.wait()
-    pack_edges(0)
-    pl.semaphore_wait(barrier, nx - 1 + 4)
-    for copy in halo_copies(0):
-        copy.start()
-
     table[...] = jnp.zeros_like(table)
     half = ((donor_rows, return_rows), (fringe_slots, hole_slots))
     for n, (first, second) in enumerate(half):
@@ -226,6 +244,13 @@
 
     lax.fori_loop(0, 2, lay_body, 0)
 
+    for load in loads:
+        load.wait()
+    pack_edges(0)
+    pl.semaphore_wait(barrier, nx - 1 + 4)
+    for copy in halo_copies(0):
+        copy.start()
+
     for now in range(STEPS):
         final = now == STEPS - 1
         f = field.at[now]
@@ -267,7 +292,7 @@
         sent[now] = mixed.reshape(64, 4, LANES)
 
         def send(step, carry):
-            to = lax.rem(q + step, nx)
+            to = peer(q, step)
             pltpu.make_async_remote_copy(
                 src_ref=sent.at[now, to],
                 dst_ref=got.at[now, q],
@@ -278,7 +303,7 @@
             ).start()
             return carry
 
-        lax.fori_loop(1, nx, send, 0)
+        lax.fori_loop(0, nx - 1, send, 0, unroll=True)
         got[now, pl.ds(q, 1)] = sent[now, pl.ds(q, 1)]
 
         for first, count, plane in GROUPS:
@@ -374,7 +399,7 @@
     by_slot = lambda rows: jnp.swapaxes(rows[0, 0], 0, 1)
     shares = lambda parts: jnp.swapaxes(parts[:, 0, 0], 1, 2)
     vmem = pl.BlockSpec(memory_space=pltpu.VMEM)
-    hbm = pl.BlockSpec(memory_space=pl.ANY)
+    hbm = pl.BlockSpec(memory_space=pltpu.HBM)
     dma = pltpu.SemaphoreType.DMA
     return pl.pallas_call(
         functools.partial(kernel, nx, ny),
@@ -382,9 +407,15 @@
             jax.ShapeDtypeStruct(background.shape, F32),
             jax.ShapeDtypeStruct(nearbody.shape, F32),
         ),
-        in_specs=[hbm, hbm] + [vmem] * 6,
+        in_specs=[hbm] * 8,
         out_specs=(vmem, vmem),
         scratch_shapes=[
+            pltpu.VMEM((2, 64), jnp.int32),
+            pltpu.VMEM((3, 2, 64), F32),
+            pltpu.VMEM((2, 64), jnp.int32),
+            pltpu.VMEM((2, 64), jnp.int32),
+            pltpu.VMEM((3, 2, 64), F32),
+            pltpu.VMEM((2, 64), jnp.int32),
             pltpu.VMEM((STEPS, PLANES, Z, LANES), F32),
             pltpu.VMEM((64, Z, LANES), F32),
             pltpu.VMEM((24, LANES), F32),
@@ -402,26 +433,30 @@
             pltpu.VMEM((STEPS, Z, LANES), F32),
             pltpu.VMEM((STEPS, 64, 4, LANES), F32),
             pltpu.VMEM((STEPS, 64, 4, LANES), F32),
-            dma((3,)),
+            dma((9,)),
             dma((STEPS, 9)),
             dma((STEPS, 9)),
             dma((STEPS,)),
             dma((STEPS,)),
-            dma((3,)),
         ],
         compiler_params=pltpu.CompilerParams(
             collective_id=0, has_side_effects=True, vmem_limit_bytes=32 * 1024 * 1024
         ),
         name="overset_steps",
     )(
-        background,
-        nearbody,
-        by_slot(donor_rows),
-        shares(donor_fractions),
-        by_slot(fringe_slots),
-        by_slot(return_rows),
-        shares(return_fractions),
-        by_slot(hole_slots),
+        *(
+            pltpu.with_memory_space_constraint(operand, pltpu.HBM)
+            for operand in (
+                background,
+                nearbody,
+                by_slot(donor_rows),
+                shares(donor_fractions),
+                by_slot(fringe_slots),
+                by_slot(return_rows),
+                shares(return_fractions),
+                by_slot(hole_slots),
+            )
+        )
     )
 
 

time: 53.4 us -> 48.5 us (0.908)
  local copies, waits for them, and re-layouts: 4.02 us -> 1.41 us
  Pallas kernels: 48.4 us -> 46.3 us
    unnamed x18 -> x2, local copies, waits for them, and re-layouts: 4.02 us -> 1.41 us
    pallas_call x1, Pallas kernels: 48.4 us -> 46.3 us  [per_device(): pl.pallas_call(functools.partial(kernel, nx, ny), out_shape=(jax.ShapeDty...]
where the time goes in v2:
time: 48.5 us; the launch traced here: 48.4 us
  Pallas kernels  46.3 us (95%)
  local copies, waits for them, and re-layouts  1.41 us (3%)
  between operations  0.64 us (1%)
    pallas_call x1, Pallas kernels, per_device(): pl.pallas_call(functools.partial(kernel, nx, ny), out_shape=(jax.ShapeDty...  46.3 us
    unnamed x2, local copies, waits for them, and re-layouts  1.41 us

profile of v2, /device:TPU:1, one launch (start us, length us, event | category | flops | bytes accessed | tf_op | source)
XLA Modules:
  0.0 48.4 jit_solution(13899697057469566011)
XLA Ops:
  0.6 46.3 %overset_steps.1 = (f32[32,16,128]{2,1,0:T(8,128)S(1)}, f32[2,16,16,128]{3,2,1,0:T(8,128)S(1)}) custom-call(f32[32,16,128]{2,1,0:T(8,128)} %back_ref.1, f32[2,16,16,128]{3,2,1,0:T(8,128)} %body_ref.1, s32[2,64]{1,0:T(2,128)} %bitcast.20, f32[3,2,64]{2,1,0:T(2,128)} %bitcast.18, s32[2,64]{1,0:T(2,128)} %bitcast.21, s32[2,64]{1,0:T(2,128)} %bitcast.22, ...), custom_call_target="tpu_custom_call" | custom-call | tf_op jit(solution)/shard_map/overset_steps/pallas_call | solution.py:404
  46.9 0.7 %copy.12 = f32[32,16,128]{2,1,0:T(8,128)} copy(f32[32,16,128]{2,1,0:T(8,128)S(1)} %get-tuple-element.4) | data formatting | bytes 524288
  47.7 0.7 %copy.13 = f32[2,16,16,128]{3,2,1,0:T(8,128)} copy(f32[2,16,16,128]{3,2,1,0:T(8,128)S(1)} %get-tuple-element.5) | data formatting | bytes 524288

commit v3 on v2

--- a/solution.py
+++ b/solution.py
@@ -78,6 +78,7 @@
     place,
     keep,
     edge,
+    corner,
     edge_above,
     edge_below,
     edge_corner,
@@ -127,7 +128,7 @@
             barrier, inc=1, device_id={"gx": there[0], "gy": there[1]}, device_id_type=MESH
         )
 
-    def halo_copies(now):
+    def halo_copies(now, which=range(9)):
         f = field.at[now]
         pairs = []
         for n, (first, count, _) in enumerate(GROUPS):
@@ -135,7 +136,7 @@
             pairs.append((f.at[first], f.at[first + count], q_down, j))
         pairs.append((edge.at[now], edge_below.at[now], q, j_up))
         pairs.append((edge.at[now], edge_above.at[now], q, j_down))
-        pairs.append((edge.at[now], edge_corner.at[now], q_down, j_down))
+        pairs.append((corner.at[now], edge_corner.at[now], q_down, j_down))
         return [
             pltpu.make_async_remote_copy(
                 src_ref=src,
@@ -145,7 +146,8 @@
                 device_id={"gx": to_q, "gy": to_j},
                 device_id_type=MESH,
             )
-            for n, (src, dst, to_q, to_j) in enumerate(pairs)
+            for n in which
+            for src, dst, to_q, to_j in pairs[n : n + 1]
         ]
 
     lane = iota((Z, LANES), 1)
@@ -159,6 +161,17 @@
                 hit = (lane == spot) | (lane == (spot - 1) % LANES)
                 packed = jnp.where(hit, rolled, packed)
         edge[now] = packed
+
+    def pack_corner(now):
+        packed = jnp.zeros((Z, LANES), F32)
+        for n, (first, _, _) in enumerate(GROUPS):
+            spot = 2 * n + 1
+            packed = jnp.where(lane == spot, pltpu.roll(field[now, first], spot, 1), packed)
+        corner[now] = packed
+
+    def start_halos(now, which):
+        for copy in halo_copies(now, which):
+            copy.start()
 
     for load in tables:
         load.wait()
@@ -204,7 +217,7 @@
     far = jnp.where(last, -1000, base + Z)
 
     def weigh(n, carry):
-        k = iota((rows, LANES), 1) + n * LANES
+        k = iota((rows, 2 * LANES), 1) + n * (2 * LANES)
         w = (
             jnp.where(k == base, w00, 0.0)
             + jnp.where(k == base + 1, w01, 0.0)
@@ -216,12 +229,18 @@
         w_low[n] = low
         return carry
 
-    lax.fori_loop(0, 8, weigh, 0)
+    lax.fori_loop(0, 4, weigh, 0)
     k = iota((rows, LANES), 1)
     near = jnp.where(last, halo_index * Z + layer_c, -1000)
-    w_halo[...] = jnp.where(k == near, w10, 0.0) + jnp.where(k == near + 1, w11, 0.0)
+    high, low = split(jnp.where(k == near, w10, 0.0) + jnp.where(k == near + 1, w11, 0.0))
+    w_halo[0] = high
+    w_halo[1] = low
     beyond = jnp.where(last, 1 + 2 * halo_index, 2 * plane_c + 2)
-    w_x[...] = jnp.where(k == 2 * plane_c, 1.0 - f1, 0.0) + jnp.where(k == beyond, f1, 0.0)
+    high, low = split(
+        jnp.where(k == 2 * plane_c, 1.0 - f1, 0.0) + jnp.where(k == beyond, f1, 0.0)
+    )
+    w_x[...] = jnp.concatenate([high, low], axis=1)
+    k = jnp.where(k < 2 * Z, k % Z, -1000)
     w_z[...] = jnp.where(k == layer_c, 1.0 - f2, 0.0) + jnp.where(k == layer_c + 1, f2, 0.0)
 
     target_i = target.astype(jnp.int32)
@@ -246,10 +265,10 @@
 
     for load in loads:
         load.wait()
+    pack_corner(0)
     pack_edges(0)
     pl.semaphore_wait(barrier, nx - 1 + 4)
-    for copy in halo_copies(0):
-        copy.start()
+    start_halos(0, (8, 1, 3, 5, 0, 2, 4, 6, 7))
 
     for now in range(STEPS):
         final = now == STEPS - 1
@@ -257,9 +276,10 @@
 
         blend = jnp.zeros((rows, LANES), F32)
         for first, count, plane in GROUPS:
-            for part in range(count // 8):
-                high, low = split(f[first + 8 * part : first + 8 * part + 8].reshape(LANES, LANES))
-                n = plane // 8 + part
+            for part in range(count // 16):
+                start = first + 16 * part
+                high, low = split(f[start : start + 16].reshape(2 * LANES, LANES))
+                n = plane // 16 + part
                 both = dot(w_high[n], jnp.concatenate([high, low], axis=1))
                 blend += both[:, :LANES] + both[:, LANES:] + dot(w_low[n], high)
 
@@ -274,17 +294,23 @@
         above = jnp.where((j == ny - 1) & in_back, zero, edge_above[now])
         even = lane % 2 == 0
         edges = jnp.where(even, above, below)
-        corner = edge_corner[now]
-        corner_back = jnp.where((j == ny - 1) | (q == nx - 1), zero, corner)
-        high_y = jnp.where(even, above, zero)
-        high_y = jnp.where(lane == 1, pltpu.roll(corner_back, 1, 1), high_y)
-        high_y = jnp.where(lane == 3, pltpu.roll(corner, LANES - 61, 1), high_y)
-        high_y = jnp.where(lane == 5, pltpu.roll(corner, LANES - 91, 1), high_y)
-
-        beyond_x = jnp.concatenate([f[33], f[51], f[69]], axis=0)
-        blend += exact_dot(w_halo[:, 0:48], beyond_x)
-        high_y = jnp.concatenate([high_y, jnp.zeros((LANES - Z, LANES), F32)], axis=0)
-        spill = exact_dot(w_x[...], high_y, ((1,), (1,)))
+        ends = (lane == 1) & ((j == ny - 1) | (q == nx - 1))
+        high, low = split(jnp.where(even, above, jnp.where(ends, zero, edge_corner[now])))
+        high_y = jnp.concatenate(
+            [
+                jnp.concatenate([high, high], axis=1),
+                jnp.concatenate([low, jnp.zeros((Z, LANES), BF16)], axis=1),
+                jnp.zeros((LANES - 2 * Z, 2 * LANES), BF16),
+            ],
+            axis=0,
+        )
+        spill = lax.dot_general(
+            w_x[...], high_y, (((1,), (1,)), ((), ())), preferred_element_type=F32
+        )
+
+        high, low = split(jnp.concatenate([f[33], f[51], f[69]], axis=0))
+        both = dot(w_halo[0, :, 0:48], jnp.concatenate([high, low], axis=1))
+        blend += both[:, :LANES] + both[:, LANES:] + dot(w_halo[1, :, 0:48], high)
         spill = jnp.sum(w_z[...] * spill, axis=1, keepdims=True)
         ahead = pltpu.roll(blend, LANES - 1, 1)
         ahead = jnp.where(iota((rows, LANES), 1) == LANES - 1, spill, ahead)
@@ -347,7 +373,7 @@
 
         high, low = split(got[now].reshape(rows, LANES))
         received = jnp.concatenate([high, low], axis=1)
-        for n in range(6):
+        for n in (0, 4, 5, 3, 1, 2):
             both = dot(place[n], received)
             added = both[:, :LANES] + both[:, LANES:]
             if n < 4:
@@ -367,10 +393,14 @@
                     first = GROUPS[n - 3][0]
                     field[now + 1, first : first + 16, 0:8] = low_part
                     field[now + 1, first : first + 16, 8:16] = new
+            if n == 5 and not final:
+                pack_corner(now + 1)
+                start_halos(now + 1, (8, 1, 3, 5, 2, 4))
+            if n == 3 and not final:
+                start_halos(now + 1, (0,))
         if not final:
             pack_edges(now + 1)
-            for copy in halo_copies(now + 1):
-                copy.start()
+            start_halos(now + 1, (6, 7))
 
     for now in range(STEPS):
         for copy in halo_copies(now):
@@ -419,14 +449,15 @@
             pltpu.VMEM((STEPS, PLANES, Z, LANES), F32),
             pltpu.VMEM((64, Z, LANES), F32),
             pltpu.VMEM((24, LANES), F32),
-            pltpu.VMEM((8, 256, LANES), BF16),
-            pltpu.VMEM((8, 256, LANES), BF16),
-            pltpu.VMEM((256, LANES), F32),
-            pltpu.VMEM((256, LANES), F32),
+            pltpu.VMEM((4, 256, 2 * LANES), BF16),
+            pltpu.VMEM((4, 256, 2 * LANES), BF16),
+            pltpu.VMEM((2, 256, LANES), BF16),
+            pltpu.VMEM((256, 2 * LANES), BF16),
             pltpu.VMEM((256, LANES), F32),
             pltpu.VMEM((256, LANES), F32),
             pltpu.VMEM((6, LANES, 256), BF16),
             pltpu.VMEM((4, LANES, LANES), F32),
+            pltpu.VMEM((STEPS, Z, LANES), F32),
             pltpu.VMEM((STEPS, Z, LANES), F32),
             pltpu.VMEM((STEPS, Z, LANES), F32),
             pltpu.VMEM((STEPS, Z, LANES), F32),

time: 48.5 us -> 47.9 us (0.988)
  Pallas kernels: 46.3 us -> 45.5 us
    pallas_call x1, Pallas kernels: 46.3 us -> 45.5 us  [per_device(): pl.pallas_call(functools.partial(kernel, nx, ny), out_shape=(jax.ShapeDty...]
where the time goes in v3:
time: 47.9 us; the launch traced here: 47.5 us
  Pallas kernels  45.5 us (95%)
  local copies, waits for them, and re-layouts  1.41 us (3%)
  between operations  0.64 us (1%)
    pallas_call x1, Pallas kernels, per_device(): pl.pallas_call(functools.partial(kernel, nx, ny), out_shape=(jax.ShapeDty...  45.5 us
    unnamed x2, local copies, waits for them, and re-layouts  1.41 us

profile of v3, /device:TPU:1, one launch (start us, length us, event | category | flops | bytes accessed | tf_op | source)
XLA Modules:
  0.0 47.5 jit_solution(13701467937098966040)
XLA Ops:
  0.6 45.5 %overset_steps.1 = (f32[32,16,128]{2,1,0:T(8,128)S(1)}, f32[2,16,16,128]{3,2,1,0:T(8,128)S(1)}) custom-call(f32[32,16,128]{2,1,0:T(8,128)} %back_ref.1, f32[2,16,16,128]{3,2,1,0:T(8,128)} %body_ref.1, s32[2,64]{1,0:T(2,128)} %bitcast.20, f32[3,2,64]{2,1,0:T(2,128)} %bitcast.18, s32[2,64]{1,0:T(2,128)} %bitcast.21, s32[2,64]{1,0:T(2,128)} %bitcast.22, ...), custom_call_target="tpu_custom_call" | custom-call | tf_op jit(solution)/shard_map/overset_steps/pallas_call | solution.py:434
  46.1 0.7 %copy.12 = f32[32,16,128]{2,1,0:T(8,128)} copy(f32[32,16,128]{2,1,0:T(8,128)S(1)} %get-tuple-element.4) | data formatting | bytes 524288
  46.8 0.7 %copy.13 = f32[2,16,16,128]{3,2,1,0:T(8,128)} copy(f32[2,16,16,128]{3,2,1,0:T(8,128)S(1)} %get-tuple-element.5) | data formatting | bytes 524288

commit v4 on v3

--- a/solution.py
+++ b/solution.py
@@ -58,8 +58,7 @@
     return_rows_ref,
     return_fractions_ref,
     hole_slots_ref,
-    back_out,
-    body_out,
+    out,
     donor_rows,
     donor_fractions,
     fringe_slots,
@@ -283,12 +282,19 @@
                 both = dot(w_high[n], jnp.concatenate([high, low], axis=1))
                 blend += both[:, :LANES] + both[:, LANES:] + dot(w_low[n], high)
 
-        for copy in halo_copies(now):
+        for copy in halo_copies(now, range(6)):
             copy.wait_recv()
 
         zero = jnp.zeros((Z, LANES), F32)
         f[0] = jnp.where(q == 0, zero, f[0])
         f[33] = jnp.where(q == nx - 1, zero, f[33])
+        high, low = split(jnp.concatenate([f[33], f[51], f[69]], axis=0))
+        both = dot(w_halo[0, :, 0:48], jnp.concatenate([high, low], axis=1))
+        blend += both[:, :LANES] + both[:, LANES:] + dot(w_halo[1, :, 0:48], high)
+        ahead = pltpu.roll(blend, LANES - 1, 1)
+
+        for copy in halo_copies(now, range(6, 9)):
+            copy.wait_recv()
         in_back = lane < 63
         below = jnp.where((j == 0) & (in_back | (lane == 127)), zero, edge_below[now])
         above = jnp.where((j == ny - 1) & in_back, zero, edge_above[now])
@@ -307,12 +313,7 @@
         spill = lax.dot_general(
             w_x[...], high_y, (((1,), (1,)), ((), ())), preferred_element_type=F32
         )
-
-        high, low = split(jnp.concatenate([f[33], f[51], f[69]], axis=0))
-        both = dot(w_halo[0, :, 0:48], jnp.concatenate([high, low], axis=1))
-        blend += both[:, :LANES] + both[:, LANES:] + dot(w_halo[1, :, 0:48], high)
         spill = jnp.sum(w_z[...] * spill, axis=1, keepdims=True)
-        ahead = pltpu.roll(blend, LANES - 1, 1)
         ahead = jnp.where(iota((rows, LANES), 1) == LANES - 1, spill, ahead)
         mixed = blend + share_y[...] * (ahead - blend)
         sent[now] = mixed.reshape(64, 4, LANES)
@@ -379,7 +380,7 @@
             if n < 4:
                 new = moved[8 * n : 8 * n + 8] + added.reshape(8, Z, LANES)
                 if final:
-                    back_out[8 * n : 8 * n + 8] = new
+                    out[8 * n : 8 * n + 8] = new
                 else:
                     field[now + 1, 1 + 8 * n : 9 + 8 * n] = new
             else:
@@ -387,8 +388,8 @@
                 low_part = moved[start : start + 16, 0:8]
                 new = moved[start : start + 16, 8:16] + added.reshape(16, 8, LANES)
                 if final:
-                    body_out[n - 4, :, 0:8] = low_part
-                    body_out[n - 4, :, 8:16] = new
+                    out[start : start + 16, 0:8] = low_part
+                    out[start : start + 16, 8:16] = new
                 else:
                     first = GROUPS[n - 3][0]
                     field[now + 1, first : first + 16, 0:8] = low_part
@@ -431,14 +432,11 @@
     vmem = pl.BlockSpec(memory_space=pltpu.VMEM)
     hbm = pl.BlockSpec(memory_space=pltpu.HBM)
     dma = pltpu.SemaphoreType.DMA
-    return pl.pallas_call(
+    fields = pl.pallas_call(
         functools.partial(kernel, nx, ny),
-        out_shape=(
-            jax.ShapeDtypeStruct(background.shape, F32),
-            jax.ShapeDtypeStruct(nearbody.shape, F32),
-        ),
+        out_shape=jax.ShapeDtypeStruct((64, Z, LANES), F32),
         in_specs=[hbm] * 8,
-        out_specs=(vmem, vmem),
+        out_specs=vmem,
         scratch_shapes=[
             pltpu.VMEM((2, 64), jnp.int32),
             pltpu.VMEM((3, 2, 64), F32),
@@ -489,6 +487,7 @@
             )
         )
     )
+    return fields[:32], fields[32:].reshape(nearbody.shape)
 
 
 def solution(mesh):

time: 47.9 us -> 47.7 us (level)
  local copies, waits for them, and re-layouts: 1.41 us -> 0.82 us
    unnamed x2 -> x0, local copies, waits for them, and re-layouts: 1.41 us -> none
    slice x0 -> x1, local copies, waits for them, and re-layouts: none -> 0.82 us  [per_device(): return (fields[:32], fields[32:].reshape(nearbody.shape))]
where the time goes in v4:
time: 47.7 us; the launch traced here: 46.9 us
  Pallas kernels  45.4 us (95%)
  local copies, waits for them, and re-layouts  0.82 us (2%)
  between operations  0.64 us (1%)
    pallas_call x1, Pallas kernels, per_device(): pl.pallas_call(functools.partial(kernel, nx, ny), out_shape=jax.ShapeDtyp...  45.4 us

profile of v4, /device:TPU:1, one launch (start us, length us, event | category | flops | bytes accessed | tf_op | source)
XLA Modules:
  0.0 46.9 jit_solution(11123327641805710391)
XLA Ops:
  0.6 45.4 %overset_steps.1 = f32[64,16,128]{2,1,0:T(8,128)S(1)} custom-call(f32[32,16,128]{2,1,0:T(8,128)} %back_ref.1, f32[2,16,16,128]{3,2,1,0:T(8,128)} %body_ref.1, s32[2,64]{1,0:T(2,128)} %bitcast.22, f32[3,2,64]{2,1,0:T(2,128)} %bitcast.20, s32[2,64]{1,0:T(2,128)} %bitcast.23, s32[2,64]{1,0:T(2,128)} %bitcast.24, f32[3,2,64]{2,1,0:T(2,128)} %bitcast.21, ...), custom_call_target="tpu_custom_call" | custom-call | tf_op jit(solution)/shard_map/overset_steps/pallas_call | solution.py:435
  46.1 0.8 %fusion = (f32[32,16,128]{2,1,0:T(8,128)}, f32[32,16,128]{2,1,0:T(8,128)}) fusion(f32[64,16,128]{2,1,0:T(8,128)S(1)} %overset_steps.1), kind=kLoop, calls=%fused_computation | loop fusion | bytes 1048576 | tf_op jit(solution)/shard_map/slice | solution.py:490
